TPU v7x, 32 devices: a whole 2x2x4 slice. The times are simulated.
32 devices in a mesh: dom: 8 (over y, x, core), rep: 4 (over z).
Axes of the slice: x: 2, y: 2, z: 4, core: 2. Of those that a mesh axis runs over, the one named last changes fastest.
Arguments:
- features: bfloat16 [32768, 512], P('dom', 'rep'), may hold values from -6 to 6
- tile_values: bfloat16 [256, 8, 128, 128], P('dom'), may hold values from -0.1875 to 0.1875
- tile_columns: int32 [256, 8], P('dom'), may hold values from 0 to 39
- boundary_rows: int32 [8, 128], P('dom'), may hold values from 0 to 4095
- train_rows: int32 [8, 4096], P('dom'), may hold values from 0 to 4095
- shuffle: int32 [8, 4096], P('dom'), may hold values from 0 to 4095, each once within a row
- labels: int32 [32768], P(('dom', 'rep')), may hold values from 0 to 152
- first_weight: bfloat16 [4, 512, 1024], replicated, may hold values from -0.125 to 0.125
- mid_weight: bfloat16 [1024, 1024], replicated, may hold values from -0.1875 to 0.1875
- out_weight: bfloat16 [1024, 153], replicated, may hold values from -0.1875 to 0.1875
Outputs:
- first_grad: float32 [4, 512, 1024], P('rep', 'dom')
- mid_grad: float32 [1024, 1024], P(('dom', 'rep'))
- out_grad: float32 [1024, 153], P(('dom', 'rep'))
Inputs may be any that keep to these rules, and one draw needn't show every extreme that they name: `tile_columns`: an entry below 32 names a block of the partition's own rows, an entry c of 32 or more names block c - 32 of the gathered boundary rows. `train_rows`: indices may repeat. `shuffle`: each row is a permutation of 0 to 4095.
All inputs are finite; a program needn't handle non-finite values.
Results may differ from a plain program's by a relative error of at most 0.02.
Values may be sent and summed in bfloat16 or wider, within the bound.
A program may use at most 128 MiB of HBM per device.

v0:
```python
import math

import jax
import jax.numpy as jnp
from jax import lax
from jax.sharding import PartitionSpec as P

HOPS = 3


root_two_pi = 0.7978845608028654
cubic_term = 0.044715


def gelu_pair(values):
    inner_arg = root_two_pi * (values + cubic_term * values * values * values)
    tanh_part = jnp.tanh(inner_arg)
    output = 0.5 * values * (1.0 + tanh_part)
    slope_out = 0.5 * (1.0 + tanh_part) + 0.5 * values * (
        1.0 - tanh_part * tanh_part
    ) * root_two_pi * (1.0 + 3.0 * cubic_term * values * values)
    return (output, slope_out)


def outer_rows(left_side, right_side):
    return lax.dot_general(
        left_side, right_side, (((0,), (0,)), ((), ())), preferred_element_type=jnp.float32
    )


def inner_cols(left_side, right_side):
    return lax.dot_general(
        left_side, right_side, (((1,), (1,)), ((), ())), preferred_element_type=jnp.float32
    )


def propagate(hop_now, bound_local, tile_columns, tile_values):
    exported = hop_now[bound_local]
    halo_rows = lax.all_gather(exported, "dom", axis=0, tiled=True)
    joined = jnp.concatenate([hop_now, halo_rows], axis=0)
    blocks = joined.reshape(-1, tile_values.shape[2], hop_now.shape[1])
    picked = blocks[tile_columns]
    summed = jnp.einsum("bkij,bkjf->bif", tile_values, picked, preferred_element_type=jnp.float32)
    return summed.reshape(hop_now.shape).astype(jnp.bfloat16)


def per_device(
    features,
    tile_values,
    tile_columns,
    boundary_rows,
    train_rows,
    shuffle,
    labels,
    first_weight,
    mid_weight,
    out_weight,
):
    hop_list = [features]
    bound_local = boundary_rows[0]
    for hop_index in range(HOPS):
        hop_list.append(propagate(hop_list[-1], bound_local, tile_columns, tile_values))
    picked_rows = train_rows[0][shuffle[0]]
    chosen = jnp.stack([hop[picked_rows] for hop in hop_list], axis=1)
    train_dev = chosen.shape[0]
    slab_width = chosen.shape[2]
    n_dom = lax.axis_size("dom")
    n_rep = lax.axis_size("rep")
    batch_rows = train_dev // n_rep
    hop_count = len(hop_list)
    quarter = hop_count * slab_width // n_dom
    hidden_width = mid_weight.shape[0]
    chosen = chosen.reshape(train_dev, 1, hop_count * slab_width)
    relayed = lax.all_to_all(
        lax.all_to_all(chosen, "dom", split_axis=0, concat_axis=0, tiled=True),
        "rep",
        split_axis=0,
        concat_axis=1,
        tiled=True,
    )
    inputs = relayed.reshape(batch_rows, n_rep * hop_count * slab_width)
    pre_first = jnp.dot(
        inputs,
        first_weight.reshape(n_rep * hop_count * slab_width, hidden_width),
        preferred_element_type=jnp.float32,
    )
    act_first, slope_first = gelu_pair(pre_first)
    act_first = act_first.astype(jnp.bfloat16)
    pre_mid = jnp.dot(act_first, mid_weight, preferred_element_type=jnp.float32)
    act_mid, slope_mid = gelu_pair(pre_mid)
    act_mid = act_mid.astype(jnp.bfloat16)
    logits = jnp.dot(act_mid, out_weight, preferred_element_type=jnp.float32)
    exp_logits = jnp.exp(logits)
    softmax_out = exp_logits / jnp.sum(exp_logits, axis=1, keepdims=True)
    classes = out_weight.shape[1]
    onehot = (labels[:, None] == jnp.arange(classes, dtype=jnp.int32)[None, :]).astype(jnp.float32)
    grad_logits = ((softmax_out - onehot) * (1.0 / math.sqrt(n_dom * train_dev))).astype(
        jnp.bfloat16
    )
    grad_mid = (inner_cols(grad_logits, out_weight) * slope_mid).astype(jnp.bfloat16)
    grad_first = (inner_cols(grad_mid, mid_weight) * slope_first).astype(jnp.bfloat16)
    columns = act_mid
    out_grad = lax.psum_scatter(
        outer_rows(columns, grad_logits), ("dom", "rep"), scatter_dimension=0, tiled=True
    )
    columns = act_first
    mid_grad = lax.psum_scatter(
        outer_rows(columns, grad_mid), ("dom", "rep"), scatter_dimension=0, tiled=True
    )
    permuted = (
        inputs.reshape(batch_rows, n_rep, n_dom, quarter)
        .transpose(0, 2, 1, 3)
        .reshape(batch_rows, n_rep * hop_count * slab_width)
    )
    columns = permuted
    first_share = lax.psum_scatter(
        outer_rows(columns, grad_first), ("dom", "rep"), scatter_dimension=0, tiled=True
    )
    return (first_share.reshape(1, quarter, hidden_width), mid_grad, out_grad)


def solution(mesh):
    placed = (
        P("dom", "rep"),
        P("dom", None, None, None),
        P("dom", None),
        P("dom", None),
        P("dom", None),
        P("dom", None),
        P(("dom", "rep")),
        P(),
        P(),
        P(),
    )
    return jax.shard_map(
        per_device,
        mesh=mesh,
        in_specs=placed,
        out_specs=(P("rep", "dom", None), P(("dom", "rep"), None), P(("dom", "rep"), None)),
        check_vma=False,
    )
```

profile of v0, /device:TPU:0, one launch (start us, length us, event | category | flops | bytes accessed | tf_op | source)
XLA Modules:
  0.0 923.6 jit_solution(209133718320304207)
XLA Ops:
  10.0 10.8 %all-gather = bf16[1024,128]{1,0:T(8,128)(2,1)S(1)} all-gather(bf16[128,128]{1,0:T(8,128)(2,1)S(1)} %gather_fusion.2), channel_id=2, replica_groups=mesh['dom'=8,'rep'=4] {'dom'}, dimensions={0}, use_global_device_ids=true | all-gather | bytes 294912 | tf_op jit(solution)/shard_map/all_gather | solution.py:39
  23.0 8.6 gather_fusion.3
  31.6 8.1 bitcast_convert_fusion.2
  40.4 9.8 %all-gather.1 = bf16[1024,128]{1,0:T(8,128)(2,1)S(1)} all-gather(bf16[128,128]{1,0:T(8,128)(2,1)S(1)} %gather_fusion.5), channel_id=3, replica_groups=mesh['dom'=8,'rep'=4] {'dom'}, dimensions={0}, use_global_device_ids=true | all-gather | bytes 294912 | tf_op jit(solution)/shard_map/all_gather | solution.py:39
  51.4 9.9 %gather_fusion.6 = bf16[256,128,128]{2,1,0:T(8,128)(2,1)} fusion(bf16[40,128,128]{2,1,0:T(8,128)(2,1)} %bitcast.76, s32[1024]{0:T(1024)S(1)} %pad_clamp_fusion), kind=kCustom, calls=%fused_computation.6 | custom fusion | bytes 16778240 | tf_op jit(solution)/shard_map/gather | solution.py:42
  61.4 9.2 bitcast_convert_fusion.1
  72.6 23.0 %gather_fusion = s32[4096]{0:T(1024)S(1)} fusion(s32[4096]{0:T(1024)S(1)} %bitcast.66, s32[4096]{0:T(1024)S(1)} %broadcast_clamp_fusion), kind=kCustom, calls=%fused_computation | custom fusion | bytes 49152 | tf_op jit(solution)/shard_map/gather | solution.py:63
  95.7 15.7 %gather_fusion.7 = bf16[4096,128]{1,0:T(8,128)(2,1)} fusion(bf16[4096,128]{1,0:T(8,128)(2,1)} %bitcast.71, s32[4096]{0:T(1024)S(1)} %broadcast_clamp_fusion.1), kind=kCustom, calls=%fused_computation.7 | custom fusion | bytes 2113536 | tf_op jit(solution)/shard_map/gather | solution.py:64
  111.4 15.0 %gather_fusion.4 = bf16[4096,128]{1,0:T(8,128)(2,1)} fusion(bf16[4096,128]{1,0:T(8,128)(2,1)S(1)} %bitcast.69, s32[4096]{0:T(1024)S(1)} %broadcast_clamp_fusion.1), kind=kCustom, calls=%fused_computation.4 | custom fusion | bytes 2113536 | tf_op jit(solution)/shard_map/gather | solution.py:64
  126.4 15.8 %gather_fusion.1 = bf16[4096,128]{1,0:T(8,128)(2,1)} fusion(bf16[4096,128]{1,0:T(8,128)(2,1)} %param.10, s32[4096]{0:T(1024)S(1)} %broadcast_clamp_fusion.1), kind=kCustom, calls=%fused_computation.1 | custom fusion | bytes 2113536 | tf_op jit(solution)/shard_map/gather | solution.py:64
  142.2 8.5 all-gather.2
  151.9 9.9 %gather_fusion.9 = bf16[256,128,128]{2,1,0:T(8,128)(2,1)} fusion(bf16[40,128,128]{2,1,0:T(8,128)(2,1)} %bitcast.75, s32[1024]{0:T(1024)S(1)} %pad_clamp_fusion), kind=kCustom, calls=%fused_computation.9 | custom fusion | bytes 16778240 | tf_op jit(solution)/shard_map/gather | solution.py:42
  161.8 8.1 bitcast_convert_fusion
  170.0 15.0 %gather_fusion.10 = bf16[4096,128]{1,0:T(8,128)(2,1)} fusion(bf16[4096,128]{1,0:T(8,128)(2,1)S(1)} %bitcast.73, s32[4096]{0:T(1024)S(1)} %broadcast_clamp_fusion.1), kind=kCustom, calls=%fused_computation.10 | custom fusion | bytes 2113536 | tf_op jit(solution)/shard_map/gather | solution.py:64
  209.0 7.8 reshape.217
  216.8 53.8 %all_to_all.20 = bf16[8,2,131072]{2,1,0:T(2,128)(2,1)} all-to-all(bf16[8,2,131072]{2,1,0:T(2,128)(2,1)} %reshape.217), channel_id=1, replica_groups=mesh['dom'=8,'rep'=4] {'dom'}, dimensions={0} | all-to-all | bytes 8388608 | tf_op jit(solution)/shard_map/all_to_all | solution.py:75
  270.6 8.7 reshape.218
  279.4 28.5 %reduce.1 = bf16[4096,512]{1,0:T(8,128)(2,1)} reduce(bf16[4096,1,512]{2,1,0:T(2,128)(2,1)} %reshape.218, bf16[]{:T(256)} %broadcast.170), dimensions={1}, to_apply=%reshape.218.reduce_sub_computation | reduce | bytes 8388610
  314.1 98.5 %all_to_all.21 = bf16[4,2,262144]{2,1,0:T(2,128)(2,1)} all-to-all(bf16[4,2,262144]{2,1,0:T(2,128)(2,1)} %reshape.219), channel_id=1, replica_groups=mesh['dom'=8,'rep'=4] {'rep'}, dimensions={0} | all-to-all | bytes 8388608 | tf_op jit(solution)/shard_map/all_to_all | solution.py:74
  432.8 7.6 fusion.25
  464.2 14.3 %fusion.14 = f32[2048,1024]{1,0:T(8,128)} fusion(bf16[1024,2048]{0,1:T(8,128)(2,1)} %bitcast.84, f32[1024,1024]{1,0:T(8,128)} %copy-done.6, bf16[1024,1024]{1,0:T(8,128)(2,1)} %copy-done.8, bf16[1024,1024]{1,0:T(8,128)(2,1)S(1)} %copy-done), kind=kOutput, calls=%fused_computation.39 | convolution fusion | flops 6462373888 | bytes 20971520 | tf_op jit(solution)/shard_map/dot_general | solution.py:26
  478.5 103.1 %reduce-scatter.8.cloned.1.call-done = f32[32,153]{1,0:T(8,128)} async-done(((f32[1024,153]{1,0:T(8,128)}), f32[32,153]{1,0:T(8,128)}) %reduce-scatter.8.cloned.1.call-update) | async-done | bytes 19600 | tf_op jit(solution)/shard_map/reduce_scatter | solution.py:103
  581.7 147.3 %reduce-scatter.6.cloned.1.call-done = f32[32,1024]{1,0:T(8,128)} async-done(((f32[1024,1024]{1,0:T(8,128)}), f32[32,1024]{1,0:T(8,128)}) %reduce-scatter.6.cloned.1.call-update) | async-done | bytes 131088 | tf_op jit(solution)/shard_map/reduce_scatter | solution.py:107
  728.9 187.7 %reduce-scatter.4.cloned.1.call-done = f32[64,1024]{1,0:T(8,128)} async-done(((f32[2048,1024]{1,0:T(8,128)}), f32[64,1024]{1,0:T(8,128)}) %reduce-scatter.4.cloned.1.call-update) | async-done | bytes 262160 | tf_op jit(solution)/shard_map/reduce_scatter | solution.py:116
  (55 shorter events, 84.4 us)
Async XLA Ops:
  7.2 433.2 %copy-start = (bf16[1024,1024]{1,0:T(8,128)(2,1)S(1)}, bf16[1024,1024]{1,0:T(8,128)(2,1)}, u32[]{:S(2)}) copy-start(bf16[1024,1024]{1,0:T(8,128)(2,1)} %param.18) | copy-start | bytes 6291460
  7.2 574.5 %reduce-scatter.8.cloned.1.call-start = ((), (), s32[]{:S(2)}) async-start(), calls=%async_computation.7 | async-start | bytes 1081344 | tf_op jit(solution)/shard_map/reduce_scatter | solution.py:103
  61.4 11.2 %copy-start.4 = (s32[1,4096]{1,0:T(1,128)S(1)}, s32[1,4096]{1,0:T(1,128)}, u32[]{:S(2)}) copy-start(s32[1,4096]{1,0:T(1,128)} %param.15) | copy-start | bytes 49156
  70.6 2.1 copy-start.1
  126.4 24.3 %copy-start.2 = (bf16[32,128,128]{1,2,0:T(8,128)(2,1)S(1)}, bf16[32,128,128]{1,2,0:T(8,128)(2,1)}, u32[]{:S(2)}) copy-start(bf16[32,128,128]{1,2,0:T(8,128)(2,1)} %bitcast_convert_fusion.1) | copy-start | bytes 3145732
  440.4 5.1 copy-start.6
  440.4 5.1 copy-start.3
  440.4 5.9 copy-start.5
  448.2 280.7 %reduce-scatter.6.cloned.1.call-start = ((), (), s32[]{:S(2)}) async-start(), calls=%async_computation.6 | async-start | bytes 4325376 | tf_op jit(solution)/shard_map/reduce_scatter | solution.py:107
  448.5 6.0 copy-start.7
  453.2 1.3 copy-start.8
  459.3 457.3 %reduce-scatter.4.cloned.1.call-start = ((), (), s32[]{:S(2)}) async-start(), calls=%async_computation.5 | async-start | bytes 8650752 | tf_op jit(solution)/shard_map/reduce_scatter | solution.py:116
Sparse Core Ops, SparseCore 0:
  448.3 133.3 reduce-scatter.7
  584.6 144.2 reduce-scatter.5
  731.9 184.6 reduce-scatter.3
where the time goes:
time: 930 us; the launch traced here: 924 us
  waiting for transfers between devices  438 us (47%)
  local copies, waits for them, and re-layouts  181 us (19%)
  blocking collectives  181 us (19%)
  matrix products  64.4 us (7%)
  other arithmetic  44.2 us (5%)
  between operations  14.4 us (2%)
    reduce_scatter x1, waiting for transfers between devices, per_device(): lax.psum_scatter(outer_rows(columns, grad_first), ('dom', 'rep'), scatter...  188 us
    reduce_scatter x1, waiting for transfers between devices, per_device(): lax.psum_scatter(outer_rows(columns, grad_mid), ('dom', 'rep'), scatter_d...  147 us
    reduce_scatter x1, waiting for transfers between devices, per_device(): lax.psum_scatter(outer_rows(columns, grad_logits), ('dom', 'rep'), scatte...  103 us
    all_to_all x1, blocking collectives, per_device(): lax.all_to_all(lax.all_to_all(chosen, 'dom', split_axis=0, concat_axis=0,...  98.5 us
    gather x4, local copies, waits for them, and re-layouts, per_device(): chosen = jnp.stack([hop[picked_rows] for hop in hop_list], axis=1)  61.5 us
    all_to_all x1, blocking collectives, per_device(): lax.all_to_all(chosen, 'dom', split_axis=0, concat_axis=0, tiled=True)  53.8 us
    unnamed x24, local copies, waits for them, and re-layouts  44.7 us
    all_gather x3, blocking collectives, propagate(): halo_rows = lax.all_gather(exported, 'dom', axis=0, tiled=True)  29.1 us
  transfers between devices with their start and end apart: 3, of which 3 were waited for; matrix products, arithmetic and copies ran while one was open for 3% of the time, Pallas kernels for 0%

commit v1 on v0

v1 whole, which is shorter than its diff:
```python
import functools
import math

import jax
import jax.numpy as jnp
from jax import lax
from jax.experimental import pallas as pl
from jax.experimental.pallas import tpu as pltpu
from jax.sharding import PartitionSpec as P

HOPS = 3
STEP_BLOCKS = 8

root_two_pi = 0.7978845608028654
cubic_term = 0.044715


def gelu_pair(values):
    inner_arg = root_two_pi * (values + cubic_term * values * values * values)
    tanh_part = jnp.tanh(inner_arg)
    output = 0.5 * values * (1.0 + tanh_part)
    slope_out = 0.5 * (1.0 + tanh_part) + 0.5 * values * (
        1.0 - tanh_part * tanh_part
    ) * root_two_pi * (1.0 + 3.0 * cubic_term * values * values)
    return (output, slope_out)


def outer_rows(left_side, right_side):
    return lax.dot_general(
        left_side, right_side, (((0,), (0,)), ((), ())), preferred_element_type=jnp.float32
    )


def inner_cols(left_side, right_side):
    return lax.dot_general(
        left_side, right_side, (((1,), (1,)), ((), ())), preferred_element_type=jnp.float32
    )


def hop_kernel(columns, hop_ref, halo_ref, tiles_ref, pick_ref, out_ref, export_ref, joined, total):
    step = pl.program_id(0)
    own_rows = hop_ref.shape[0]
    _, fan_in, tile, _ = tiles_ref.shape

    @pl.when(step == 0)
    def _():
        joined[:own_rows] = hop_ref[...]
        joined[own_rows:] = halo_ref[...]
        total[...] = jnp.zeros_like(total)

    for block in range(STEP_BLOCKS):
        row = step * STEP_BLOCKS + block
        left = jnp.concatenate([tiles_ref[block, k] for k in range(fan_in)], axis=1)
        right = jnp.concatenate(
            [
                joined[pl.ds(pl.multiple_of(columns[row, k] * tile, tile), tile)]
                for k in range(fan_in)
            ],
            axis=0,
        )
        summed = jnp.dot(left, right, preferred_element_type=jnp.float32)
        out_ref[block * tile : (block + 1) * tile] = summed.astype(out_ref.dtype)
    total[...] += jnp.dot(pick_ref[...], out_ref[...], preferred_element_type=jnp.float32)

    @pl.when(step == pl.num_programs(0) - 1)
    def _():
        export_ref[...] = total[...].astype(export_ref.dtype)


def propagate(hop_now, halo_rows, tile_columns, tile_values, pick_boundary):
    rows, width = hop_now.shape
    blocks, fan_in, tile, _ = tile_values.shape
    exported = pick_boundary.shape[0]
    step_rows = STEP_BLOCKS * tile
    whole = lambda step, columns: (0, 0)
    return pl.pallas_call(
        hop_kernel,
        grid_spec=pltpu.PrefetchScalarGridSpec(
            num_scalar_prefetch=1,
            grid=(blocks // STEP_BLOCKS,),
            in_specs=[
                pl.BlockSpec((rows, width), whole),
                pl.BlockSpec(halo_rows.shape, whole),
                pl.BlockSpec(
                    (STEP_BLOCKS, fan_in, tile, tile), lambda step, columns: (step, 0, 0, 0)
                ),
                pl.BlockSpec((exported, step_rows), lambda step, columns: (0, step)),
            ],
            out_specs=[
                pl.BlockSpec((step_rows, width), lambda step, columns: (step, 0)),
                pl.BlockSpec((exported, width), whole),
            ],
            scratch_shapes=[
                pltpu.VMEM((rows + halo_rows.shape[0], width), jnp.bfloat16),
                pltpu.VMEM((exported, width), jnp.float32),
            ],
        ),
        out_shape=[
            jax.ShapeDtypeStruct((rows, width), jnp.bfloat16),
            jax.ShapeDtypeStruct((exported, width), jnp.bfloat16),
        ],
        compiler_params=pltpu.CompilerParams(vmem_limit_bytes=40 * 1024 * 1024),
        cost_estimate=pl.CostEstimate(
            flops=2 * blocks * fan_in * tile * tile * width,
            bytes_accessed=2 * (tile_values.size + 4 * rows * width),
            transcendentals=0,
        ),
        name="propagate_hop",
    )(tile_columns, hop_now, halo_rows, tile_values, pick_boundary)


def to_rows(hop_now, n_rep):
    rows, width = hop_now.shape
    sent = hop_now.reshape(n_rep, rows // n_rep, width)
    return lax.all_to_all(sent, "rep", split_axis=0, concat_axis=0, tiled=True)


def per_device(
    features,
    tile_values,
    tile_columns,
    boundary_rows,
    train_rows,
    shuffle,
    labels,
    first_weight,
    mid_weight,
    out_weight,
):
    n_dom = lax.axis_size("dom")
    n_rep = lax.axis_size("rep")
    rows, width = features.shape
    train_dev = shuffle.shape[1]
    batch_rows = rows // n_rep
    hidden = mid_weight.shape[0]
    classes = out_weight.shape[1]
    hop_count = HOPS + 1

    bound = boundary_rows[0]
    pick_boundary = (bound[:, None] == jnp.arange(rows, dtype=jnp.int32)[None, :]).astype(
        jnp.bfloat16
    )

    hop_now = features
    exported = features[bound]
    moved = [to_rows(hop_now, n_rep)]
    for hop_index in range(HOPS):
        halo_rows = lax.all_gather(exported, "dom", axis=0, tiled=True)
        hop_now, exported = propagate(
            hop_now, halo_rows, tile_columns, tile_values, pick_boundary
        )
        moved.append(to_rows(hop_now, n_rep))

    all_labels = lax.all_gather(labels, ("dom", "rep"), axis=0, tiled=True)
    own_labels = lax.dynamic_index_in_dim(
        all_labels.reshape(n_dom, n_dom, train_dev // n_dom),
        lax.axis_index("dom"),
        axis=1,
        keepdims=False,
    ).reshape(train_dev)
    picked_rows = train_rows[0][shuffle[0]] - lax.axis_index("rep") * batch_rows
    paper_hot = (
        picked_rows[:, None] == jnp.arange(batch_rows, dtype=jnp.int32)[None, :]
    ).astype(jnp.bfloat16)
    label_hot = (own_labels[:, None] == jnp.arange(classes, dtype=jnp.int32)[None, :]).astype(
        jnp.bfloat16
    )
    counts = outer_rows(paper_hot, label_hot)
    times = jnp.sum(counts, axis=1, keepdims=True)

    pre_first = None
    columns = []
    for hop_index in range(hop_count):
        part = moved[hop_index].transpose(1, 0, 2).reshape(batch_rows, n_rep * width)
        columns.append(part)
        weight = first_weight[:, hop_index * width : (hop_index + 1) * width].reshape(
            n_rep * width, hidden
        )
        term = jnp.dot(part, weight, preferred_element_type=jnp.float32)
        pre_first = term if pre_first is None else pre_first + term
    act_first, slope_first = gelu_pair(pre_first)
    act_first = act_first.astype(jnp.bfloat16)
    pre_mid = jnp.dot(act_first, mid_weight, preferred_element_type=jnp.float32)
    act_mid, slope_mid = gelu_pair(pre_mid)
    act_mid = act_mid.astype(jnp.bfloat16)
    logits = jnp.dot(act_mid, out_weight, preferred_element_type=jnp.float32)
    exp_logits = jnp.exp(logits)
    softmax_out = exp_logits / jnp.sum(exp_logits, axis=1, keepdims=True)
    grad_logits = jnp.where(times > 0.0, softmax_out * times - counts, 0.0)
    grad_logits = (grad_logits * (1.0 / math.sqrt(n_dom * train_dev))).astype(jnp.bfloat16)
    grad_mid = (inner_cols(grad_logits, out_weight) * slope_mid).astype(jnp.bfloat16)

    def share(full, lead):
        part = lax.psum_scatter(full, "dom", scatter_dimension=lead, tiled=True)
        return lax.psum_scatter(part, "rep", scatter_dimension=0, tiled=True)

    out_share = outer_rows(act_mid, grad_logits).astype(jnp.bfloat16)
    out_share = out_share.reshape(n_dom, n_rep, hidden // (n_dom * n_rep), classes)
    out_share = lax.psum_scatter(out_share, "dom", scatter_dimension=0, tiled=False)
    out_share = lax.psum_scatter(out_share, "rep", scatter_dimension=0, tiled=False)
    mid_share = outer_rows(act_first, grad_mid).astype(jnp.bfloat16)
    mid_share = mid_share.reshape(n_dom, n_rep, hidden // (n_dom * n_rep), hidden)
    mid_share = lax.psum_scatter(mid_share, "dom", scatter_dimension=0, tiled=False)
    mid_share = lax.psum_scatter(mid_share, "rep", scatter_dimension=0, tiled=False)

    grad_first = (inner_cols(grad_mid, mid_weight) * slope_first).astype(jnp.bfloat16)
    first_parts = [
        outer_rows(part, grad_first).astype(jnp.bfloat16).reshape(n_rep, width, hidden)
        for part in columns
    ]
    first_share = jnp.concatenate(first_parts, axis=1)
    quarter = hop_count * width // n_dom
    first_share = share(first_share, 1)
    return (
        first_share.astype(jnp.float32).reshape(1, quarter, hidden),
        mid_share.astype(jnp.float32),
        out_share.astype(jnp.float32),
    )


def solution(mesh):
    placed = (
        P("dom", "rep"),
        P("dom", None, None, None),
        P("dom", None),
        P("dom", None),
        P("dom", None),
        P("dom", None),
        P(("dom", "rep")),
        P(),
        P(),
        P(),
    )
    return jax.shard_map(
        per_device,
        mesh=mesh,
        in_specs=placed,
        out_specs=(P("rep", "dom", None), P(("dom", "rep"), None), P(("dom", "rep"), None)),
        check_vma=False,
    )
```

time: 930 us -> 465 us (0.50)
  waiting for transfers between devices: 438 us -> 170 us
  local copies, waits for them, and re-layouts: 181 us -> 48.1 us
  blocking collectives: 181 us -> 143 us
  other arithmetic: 44.2 us -> 8.54 us
  Pallas kernels: 0 us -> 14.4 us
  starting transfers between devices: 0.37 us -> 14 us
  matrix products: 64.4 us -> 51.1 us
    reduce_scatter x3 -> x6, waiting for transfers between devices: 438 us -> 161 us  [the longest x1 54.6 us: share(): part = lax.psum_scatter(full, 'dom', scatter_dimension=lead, tiled=True)]
    all_to_all x2 -> x1, blocking collectives: 152 us -> 31.2 us  [to_rows(): return lax.all_to_all(sent, 'rep', split_axis=0, concat_axis=0, tiled=True)]
    gather x11 -> x2, local copies, waits for them, and re-layouts: 118 us -> 25 us  [the longest x1 23 us: per_device(): picked_rows = train_rows[0][shuffle[0]] - lax.axis_index('rep') * batch_rows]
    all_gather x3 -> x4, blocking collectives: 29.1 us -> 112 us  [the longest x1 83.5 us: per_device(): all_labels = lax.all_gather(labels, ('dom', 'rep'), axis=0, tiled=True)]
    unnamed x24 -> x49, local copies, waits for them, and re-layouts: 44.7 us -> 12.8 us
    unnamed x1 -> x0, other arithmetic: 28.5 us -> none
    dot_general x4, matrix products: 33 us -> 18.5 us  [per_device(): term = jnp.dot(part, weight, preferred_element_type=jnp.float32)]
    pallas_call x0 -> x3, Pallas kernels: none -> 14.4 us  [propagate(): pl.pallas_call(hop_kernel, grid_spec=pltpu.PrefetchScalarGridSpec(num_sca...]
  transfers between devices with their start and end apart: 3 -> 9, of which waited for: 3 -> 7; matrix products, arithmetic and copies ran while one was open for 3% -> 16% of each run, Pallas kernels for 0% -> 1%
where the time goes in v1:
time: 465 us; the launch traced here: 464 us
  waiting for transfers between devices  170 us (37%)
  blocking collectives  143 us (31%)
  matrix products  51.1 us (11%)
  local copies, waits for them, and re-layouts  48.1 us (10%)
  between operations  14.5 us (3%)
  Pallas kernels  14.4 us (3%)
  starting transfers between devices  14 us (3%)
  other arithmetic  8.54 us (2%)
    all_gather x1, blocking collectives, per_device(): all_labels = lax.all_gather(labels, ('dom', 'rep'), axis=0, tiled=True)  83.5 us
    reduce_scatter x1, waiting for transfers between devices, share(): part = lax.psum_scatter(full, 'dom', scatter_dimension=lead, tiled=True)  54.6 us
    reduce_scatter x1, waiting for transfers between devices, per_device(): lax.psum_scatter(mid_share, 'dom', scatter_dimension=0, tiled=False)  44.8 us
    all_to_all x1, blocking collectives, to_rows(): return lax.all_to_all(sent, 'rep', split_axis=0, concat_axis=0, tiled=True)  31.2 us
    all_gather x3, blocking collectives, per_device(): halo_rows = lax.all_gather(exported, 'dom', axis=0, tiled=True)  28.4 us
    gather x1, local copies, waits for them, and re-layouts, per_device(): picked_rows = train_rows[0][shuffle[0]] - lax.axis_index('rep') * batch_rows  23 us
    reduce_scatter x1, waiting for transfers between devices, per_device(): lax.psum_scatter(out_share, 'rep', scatter_dimension=0, tiled=False)  21.2 us
    reduce_scatter x1, waiting for transfers between devices, share(): return lax.psum_scatter(part, 'rep', scatter_dimension=0, tiled=True)  20.7 us
  transfers between devices with their start and end apart: 9, of which 7 were waited for; matrix products, arithmetic and copies ran while one was open for 16% of the time, Pallas kernels for 1%

profile of v1, /device:TPU:0, one launch (start us, length us, event | category | flops | bytes accessed | tf_op | source)
XLA Modules:
  0.0 463.7 jit_solution(13681703802813778562)
XLA Ops:
  11.7 10.8 %all-gather.halo_ref = bf16[1024,128]{1,0:T(8,128)(2,1)S(1)} all-gather(bf16[128,128]{1,0:T(8,128)(2,1)S(1)} %gather_fusion.1), channel_id=2, replica_groups=mesh['dom'=8,'rep'=4] {'dom'}, dimensions={0}, use_global_device_ids=true | all-gather | bytes 294912 | tf_op jit(solution)/shard_map/all_gather | solution.py:148
  27.1 4.6 propagate_hop.3
  31.7 9.3 %all_gather.14.halo_ref = bf16[1024,128]{1,0:T(8,128)(2,1)S(1)} all-gather(bf16[128,128]{1,0:T(8,128)(2,1)S(1)} %get-tuple-element.9), channel_id=1, replica_groups=mesh['dom'=8,'rep'=4] {'dom'}, dimensions={0}, use_global_device_ids=true | all-gather | bytes 294912 | tf_op jit(solution)/shard_map/all_gather | solution.py:148
  41.0 4.6 propagate_hop.4
  45.6 31.2 %all_to_all.20 = bf16[4,1024,128]{2,1,0:T(8,128)(2,1)} all-to-all(bf16[4,1024,128]{2,1,0:T(8,128)(2,1)S(1)} %bitcast.77), channel_id=1, replica_groups=mesh['dom'=8,'rep'=4] {'rep'}, dimensions={0} | all-to-all | bytes 2097152 | tf_op jit(solution)/shard_map/all_to_all | solution.py:115
  77.7 4.3 all-to-all-start.1
  82.0 83.5 %all_gather.12 = s32[32768]{0:T(1024)S(1)} all-gather(s32[1024]{0:T(1024)S(1)} %copy-done.22), channel_id=1, replica_groups=mesh['dom'=8,'rep'=4] {'dom','rep'}, dimensions={0}, use_global_device_ids=true | all-gather | bytes 135168 | tf_op jit(solution)/shard_map/all_gather | solution.py:154
  169.9 23.0 %gather_fusion = s32[4096]{0:T(1024)S(1)} fusion(s32[4096]{0:T(1024)S(1)} %bitcast.80, s32[4096]{0:T(1024)S(1)} %broadcast_clamp_fusion), kind=kCustom, calls=%fused_computation | custom fusion | bytes 49152 | tf_op jit(solution)/shard_map/gather | solution.py:161
  192.9 8.3 %all_gather.15.halo_ref = bf16[1024,128]{1,0:T(8,128)(2,1)S(1)} all-gather(bf16[128,128]{1,0:T(8,128)(2,1)S(1)} %get-tuple-element.11), channel_id=1, replica_groups=mesh['dom'=8,'rep'=4] {'dom'}, dimensions={0}, use_global_device_ids=true | all-gather | bytes 294912 | tf_op jit(solution)/shard_map/all_gather | solution.py:148
  205.9 5.2 %propagate_hop.5 = (bf16[4096,128]{1,0:T(8,128)(2,1)S(1)}, bf16[128,128]{1,0:T(8,128)(2,1)}) custom-call(s32[32,8]{1,0:T(8,128)S(1)} %copy.33.columns, bf16[4096,128]{1,0:T(8,128)(2,1)S(1)} %copy-done.6, bf16[1024,128]{1,0:T(8,128)(2,1)S(1)} %all_gather.15.halo_ref, bf16[32,8,128,128]{3,2,1,0:T(8,128)(2,1)S(1)} %copy-done.3, ...), custom_call_target="tpu_custom_call" | custom-call | flops 1073741824 | bytes 12582912 | tf_op jit(solution)/shard_map/propagate_hop/pallas_call | solution.py:76
  212.1 5.0 %all-to-all-start.3 = ((bf16[4,1024,128]{2,1,0:T(8,128)(2,1)}), bf16[4,1024,128]{2,1,0:T(8,128)(2,1)S(1)}, u32[]{:S(2)}, u32[]{:S(2)}) async-start(bf16[4,1024,128]{2,1,0:T(8,128)(2,1)} %bitcast.79), calls=%async_computation.3 | async-start | bytes 2097152 | tf_op jit(solution)/shard_map/all_to_all | solution.py:115
  217.2 4.6 fusion.31
  225.0 4.5 fusion.21
  229.5 4.5 fusion.23
  234.0 9.4 %all-to-all-done.3 = bf16[4,1024,128]{2,1,0:T(8,128)(2,1)S(1)} async-done(((bf16[4,1024,128]{2,1,0:T(8,128)(2,1)}), bf16[4,1024,128]{2,1,0:T(8,128)(2,1)S(1)}, u32[]{:S(2)}, u32[]{:S(2)}) %all-to-all-start.3) | async-done | bytes 1048608 | tf_op jit(solution)/shard_map/all_to_all | solution.py:115
  243.4 6.3 %bitcast_add_fusion = f32[1024,1024]{1,0:T(8,128)S(1)} fusion(f32[1024,1024,1]{1,0,2:T(8,128)} %fusion.19, f32[1024,1024,1]{1,0,2:T(8,128)} %fusion.21, f32[1024,1024,1]{1,0,2:T(8,128)} %fusion.23, bf16[4,512,1024]{2,1,0:T(8,128)(2,1)} %param.17, bf16[4,1024,128]{2,1,0:T(8,128)(2,1)S(1)} %all-to-all-done.3), kind=kOutput, calls=%fused_computation.24 | convolution fusion | flops 1076887552 | bytes 18874368 | tf_op jit(solution)/shard_map/dot_general | solution.py:179
  249.7 5.1 %multiply_convert_fusion = (bf16[1024,1024]{1,0:T(8,128)(2,1)S(1)}, f32[1024,1024]{1,0:T(8,128)}) fusion(bf16[1024,1024]{1,0:T(8,128)(2,1)S(1)} %copy-done, f32[1024,1024]{1,0:T(8,128)S(1)} %bitcast_add_fusion), kind=kOutput, calls=%fused_computation.27 | convolution fusion | flops 2166358016 | bytes 12582912 | tf_op jit(solution)/shard_map/dot_general | solution.py:183
  260.2 4.7 %fusion.10 = bf16[1024,1024]{1,0:T(8,128)(2,1)S(1)} fusion(f32[1024,1024]{1,0:T(8,128)} %get-tuple-element.14, bf16[1024,153]{0,1:T(8,128)(2,1)} %copy-done.19, bf16[1024,153]{0,1:T(8,128)(2,1)S(1)} %copy-done.18), kind=kOutput, calls=%fused_computation.17 | convolution fusion | flops 340787200 | bytes 6918144 | tf_op jit(solution)/shard_map/dot_general | solution.py:35
  277.4 6.9 %fusion.15 = bf16[1024,1024]{1,0:T(8,128)(2,1)S(1)} fusion(f32[1024,1024]{1,0:T(8,128)} %copy-done.11, bf16[1024,1024]{1,0:T(8,128)(2,1)} %copy-done.23, bf16[1024,1024]{1,0:T(8,128)(2,1)S(1)} %copy-done), kind=kOutput, calls=%fused_computation.22 | convolution fusion | flops 2167406592 | bytes 10485760 | tf_op jit(solution)/shard_map/dot_general | solution.py:35
  292.4 44.8 %reduce-scatter.11.cloned.1.call-done = bf16[1,4,32,1024]{3,2,1,0:T(8,128)(2,1)} async-done(((bf16[8,4,32,1024]{3,2,1,0:T(8,128)(2,1)}), bf16[1,4,32,1024]{3,2,1,0:T(8,128)(2,1)}) %reduce-scatter.11.cloned.1.call-update) | async-done | bytes 262160 | tf_op jit(solution)/shard_map/reduce_scatter | solution.py:203
  337.3 54.6 %reduce-scatter.7.cloned.1.call-done = bf16[4,64,1024]{2,1,0:T(8,128)(2,1)} async-done(((bf16[4,512,1024]{2,1,0:T(8,128)(2,1)}), bf16[4,64,1024]{2,1,0:T(8,128)(2,1)}) %reduce-scatter.7.cloned.1.call-update) | async-done | bytes 524304 | tf_op jit(solution)/shard_map/reduce_scatter | solution.py:194
  392.0 21.2 %reduce-scatter.17.cloned.1.call-done = bf16[1,32,153]{2,1,0:T(8,128)(2,1)} async-done(((bf16[4,32,153]{2,1,0:T(8,128)(2,1)}), bf16[1,32,153]{2,1,0:T(8,128)(2,1)}) %reduce-scatter.17.cloned.1.call-update) | async-done | bytes 9808 | tf_op jit(solution)/shard_map/reduce_scatter | solution.py:200
  414.4 18.6 %reduce-scatter.13.cloned.1.call-done = bf16[1,32,1024]{2,1,0:T(8,128)(2,1)} async-done(((bf16[4,32,1024]{2,1,0:T(8,128)(2,1)}), bf16[1,32,1024]{2,1,0:T(8,128)(2,1)}) %reduce-scatter.13.cloned.1.call-update) | async-done | bytes 65552 | tf_op jit(solution)/shard_map/reduce_scatter | solution.py:204
  434.5 20.7 %reduce-scatter.9.cloned.1.call-done = bf16[1,64,1024]{2,1,0:T(8,128)(2,1)} async-done(((bf16[4,64,1024]{2,1,0:T(8,128)(2,1)}), bf16[1,64,1024]{2,1,0:T(8,128)(2,1)}) %reduce-scatter.9.cloned.1.call-update) | async-done | bytes 131088 | tf_op jit(solution)/shard_map/reduce_scatter | solution.py:195
  (93 shorter events, 53.5 us)
Async XLA Ops:
  7.2 242.5 %copy-start = (bf16[1024,1024]{1,0:T(8,128)(2,1)S(1)}, bf16[1024,1024]{1,0:T(8,128)(2,1)}, u32[]{:S(2)}) copy-start(bf16[1024,1024]{1,0:T(8,128)(2,1)} %param.18) | copy-start | bytes 6291460
  22.5 3.4 copy-start.1
  27.1 13.9 %copy-start.2 = (bf16[32,8,128,128]{3,2,1,0:T(8,128)(2,1)S(1)}, bf16[32,8,128,128]{3,2,1,0:T(8,128)(2,1)}, u32[]{:S(2)}) copy-start(bf16[32,8,128,128]{3,2,1,0:T(8,128)(2,1)} %tiles_ref.5) | copy-start | bytes 25165828
  31.7 13.9 %copy-start.7 = (bf16[4096,128]{1,0:T(8,128)(2,1)}, bf16[4096,128]{1,0:T(8,128)(2,1)S(1)}, u32[]{:S(2)}) copy-start(bf16[4096,128]{1,0:T(8,128)(2,1)S(1)} %get-tuple-element.8.hop_ref) | copy-start | bytes 3145732
  45.6 36.5 %copy-start.22 = (s32[1024]{0:T(1024)S(1)}, s32[1024]{0:T(1024)}, u32[]{:S(2)}) copy-start(s32[1024]{0:T(1024)} %param.16) | copy-start | bytes 12292
  45.6 124.3 %copy-start.21 = (s32[1,4096]{1,0:T(1,128)S(1)}, s32[1,4096]{1,0:T(1,128)}, u32[]{:S(2)}) copy-start(s32[1,4096]{1,0:T(1,128)} %param.15) | copy-start | bytes 49156
  45.6 124.3 %copy-start.9 = (s32[1,4096]{1,0:T(1,128)S(1)}, s32[1,4096]{1,0:T(1,128)}, u32[]{:S(2)}) copy-start(s32[1,4096]{1,0:T(1,128)} %param.14) | copy-start | bytes 49156
  77.7 87.8 %all-to-all-start.1 = ((bf16[4,1024,128]{2,1,0:T(8,128)(2,1)}), bf16[4,1024,128]{2,1,0:T(8,128)(2,1)}, u32[]{:S(2)}, u32[]{:S(2)}) async-start(bf16[4,1024,128]{2,1,0:T(8,128)(2,1)} %bitcast.78), calls=%async_computation.1 | async-start | bytes 2097152 | tf_op jit(solution)/shard_map/all_to_all | solution.py:115
  165.6 46.5 %all-to-all-start = ((bf16[4,1024,128]{2,1,0:T(8,128)(2,1)}), bf16[4,1024,128]{2,1,0:T(8,128)(2,1)}, u32[]{:S(2)}, u32[]{:S(2)}) async-start(bf16[4,1024,128]{2,1,0:T(8,128)(2,1)} %bitcast.76), calls=%async_computation | async-start | bytes 2097152 | tf_op jit(solution)/shard_map/all_to_all | solution.py:115
  212.1 31.3 %all-to-all-start.3 = ((bf16[4,1024,128]{2,1,0:T(8,128)(2,1)}), bf16[4,1024,128]{2,1,0:T(8,128)(2,1)S(1)}, u32[]{:S(2)}, u32[]{:S(2)}) async-start(bf16[4,1024,128]{2,1,0:T(8,128)(2,1)} %bitcast.79), calls=%async_computation.3 | async-start | bytes 2097152 | tf_op jit(solution)/shard_map/all_to_all | solution.py:115
  217.2 75.2 %reduce-scatter.15.cloned.1.call-start = ((), (), s32[]{:S(2)}) async-start(), calls=%async_computation.14 | async-start | bytes 589824 | tf_op jit(solution)/shard_map/reduce_scatter | solution.py:199
  217.2 4.6 copy-start.10
  217.2 4.6 copy-start.20
  249.7 5.1 %copy-start.11 = (f32[1024,1024]{1,0:T(8,128)}, f32[1024,1024]{1,0:T(8,128)S(1)}, u32[]{:S(2)}) copy-start(f32[1024,1024]{1,0:T(8,128)S(1)} %bitcast_add_fusion) | copy-start | bytes 12582916
  249.7 5.1 %copy-start.18 = (bf16[1024,153]{0,1:T(8,128)(2,1)S(1)}, bf16[1024,153]{0,1:T(8,128)(2,1)}, u32[]{:S(2)}) copy-start(bf16[1024,153]{0,1:T(8,128)(2,1)} %param.19) | copy-start | bytes 940036
  249.7 5.9 %copy-start.17 = (f32[1024,153]{0,1:T(8,128)S(1)}, f32[1024,153]{0,1:T(8,128)}, u32[]{:S(2)}) copy-start(f32[1024,153]{0,1:T(8,128)} %get-tuple-element.16) | copy-start | bytes 1880068
  259.9 77.3 %reduce-scatter.11.cloned.1.call-start = ((), (), s32[]{:S(2)}) async-start(), calls=%async_computation.12 | async-start | bytes 2359296 | tf_op jit(solution)/shard_map/reduce_scatter | solution.py:203
  260.2 4.8 %copy-start.12 = (f32[1024,1024]{1,0:T(8,128)S(1)}, f32[1024,1024]{1,0:T(8,128)}, u32[]{:S(2)}) copy-start(f32[1024,1024]{1,0:T(8,128)} %copy-done.11) | copy-start | bytes 12582916
  264.9 4.2 copy-start.23
  269.1 122.8 %reduce-scatter.7.cloned.1.call-start = ((), (), s32[]{:S(2)}) async-start(), calls=%async_computation.10 | async-start | bytes 4718592 | tf_op jit(solution)/shard_map/reduce_scatter | solution.py:194
  277.4 7.0 %copy-start.13 = (bf16[1024,4,128]{0,2,1:T(8,128)(2,1)S(1)}, bf16[1024,4,128]{0,2,1:T(8,128)(2,1)}, u32[]{:S(2)}) copy-start(bf16[1024,4,128]{0,2,1:T(8,128)(2,1)} %copy.37) | copy-start | bytes 3145732
  291.7 121.5 %reduce-scatter.17.cloned.1.call-start = ((), (), s32[]{:S(2)}) async-start(), calls=%async_computation.15 | async-start | bytes 81920 | tf_op jit(solution)/shard_map/reduce_scatter | solution.py:200
  292.3 140.7 %reduce-scatter.13.cloned.1.call-start = ((), (), s32[]{:S(2)}) async-start(), calls=%async_computation.13 | async-start | bytes 327680 | tf_op jit(solution)/shard_map/reduce_scatter | solution.py:204
  337.2 118.0 %reduce-scatter.9.cloned.1.call-start = ((), (), s32[]{:S(2)}) async-start(), calls=%async_computation.11 | async-start | bytes 655360 | tf_op jit(solution)/shard_map/reduce_scatter | solution.py:195
  (9 other events, 12.5 us)
Sparse Core Ops, SparseCore 0:
  260.0 32.2 reduce-scatter.14
  296.0 41.2 reduce-scatter.10
  340.6 51.3 reduce-scatter.6
  394.1 18.9 reduce-scatter.16
  415.2 17.7 reduce-scatter.12
  435.2 19.9 reduce-scatter.8

commit v2 on v1

--- a/solution.py
+++ b/solution.py
@@ -109,10 +109,46 @@
     )(tile_columns, hop_now, halo_rows, tile_values, pick_boundary)
 
 
-def to_rows(hop_now, n_rep):
-    rows, width = hop_now.shape
-    sent = hop_now.reshape(n_rep, rows // n_rep, width)
+def exchange_rows(sent):
     return lax.all_to_all(sent, "rep", split_axis=0, concat_axis=0, tiled=True)
+
+
+def halve(part, name, bit, axis):
+    size = lax.axis_size(name)
+    mine = (lax.axis_index(name) >> bit) & 1
+    kept = lax.dynamic_index_in_dim(part, mine, axis, keepdims=False)
+    sent = lax.dynamic_index_in_dim(part, 1 - mine, axis, keepdims=False)
+    pairs = [(i, i ^ (1 << bit)) for i in range(size)]
+    came = lax.ppermute(sent, name, pairs)
+    return kept.astype(jnp.float32) + came.astype(jnp.float32)
+
+
+def scatter_sum(part, bits, order):
+    rows, cols = part.shape[-2:]
+    left = list(bits)
+    for bit in order:
+        axis = 1 + left.index(bit)
+        part = halve(part, "dom", bit, axis).astype(jnp.bfloat16)
+        left.remove(bit)
+    rep_bits = part.shape[0].bit_length() - 1
+    part = part.reshape((2,) * rep_bits + (rows, cols))
+    for bit in range(rep_bits):
+        part = part.astype(jnp.bfloat16)
+        part = halve(part, "rep", bit, rep_bits - 1 - bit)
+    return part
+
+
+def scatter_two_ways(part, dom_bits):
+    n_rep, _, rows, cols = part.shape
+    bits = list(range(dom_bits - 1, 0, -1))
+    part = part.reshape((n_rep,) + (2,) * len(bits) + (rows, cols))
+    rest = bits[::-1]
+    middle = len(rest) // 2
+    shares = [
+        scatter_sum(part[..., : cols // 2], bits, rest),
+        scatter_sum(part[..., cols // 2 :], bits, rest[middle:] + rest[:middle]),
+    ]
+    return jnp.concatenate(shares, axis=-1)
 
 
 def per_device(
@@ -141,23 +177,36 @@
         jnp.bfloat16
     )
 
+    label_rows = labels.astype(jnp.bfloat16).reshape(-1, width)
+    lines = label_rows.shape[0]
+    label_rows = jnp.concatenate([label_rows, label_rows], axis=0)
+    riders = jnp.broadcast_to(label_rows[None], (n_rep,) + label_rows.shape)
     hop_now = features
     exported = features[bound]
-    moved = [to_rows(hop_now, n_rep)]
+    first_rows = exchange_rows(
+        jnp.concatenate([hop_now.reshape(n_rep, batch_rows, width), riders], axis=1)
+    )
+    moved = [first_rows[:, :batch_rows]]
+    part_labels = first_rows[:, batch_rows : batch_rows + lines].reshape(n_rep * lines, width)
+    borders = bound.shape[0]
     for hop_index in range(HOPS):
-        halo_rows = lax.all_gather(exported, "dom", axis=0, tiled=True)
+        if hop_index == HOPS - 1:
+            gathered = lax.all_gather(jnp.concatenate([exported, part_labels], axis=0), "dom")
+            halo_rows = gathered[:, :borders].reshape(n_dom * borders, width)
+            all_labels = gathered[:, borders:]
+        else:
+            halo_rows = lax.all_gather(exported, "dom", axis=0, tiled=True)
         hop_now, exported = propagate(
             hop_now, halo_rows, tile_columns, tile_values, pick_boundary
         )
-        moved.append(to_rows(hop_now, n_rep))
-
-    all_labels = lax.all_gather(labels, ("dom", "rep"), axis=0, tiled=True)
+        moved.append(exchange_rows(hop_now.reshape(n_rep, batch_rows, width)))
+
     own_labels = lax.dynamic_index_in_dim(
         all_labels.reshape(n_dom, n_dom, train_dev // n_dom),
         lax.axis_index("dom"),
         axis=1,
         keepdims=False,
-    ).reshape(train_dev)
+    ).reshape(train_dev).astype(jnp.int32)
     picked_rows = train_rows[0][shuffle[0]] - lax.axis_index("rep") * batch_rows
     paper_hot = (
         picked_rows[:, None] == jnp.arange(batch_rows, dtype=jnp.int32)[None, :]
@@ -190,31 +239,30 @@
     grad_logits = (grad_logits * (1.0 / math.sqrt(n_dom * train_dev))).astype(jnp.bfloat16)
     grad_mid = (inner_cols(grad_logits, out_weight) * slope_mid).astype(jnp.bfloat16)
 
-    def share(full, lead):
-        part = lax.psum_scatter(full, "dom", scatter_dimension=lead, tiled=True)
-        return lax.psum_scatter(part, "rep", scatter_dimension=0, tiled=True)
+    dom_bits = n_dom.bit_length() - 1
+    quarter = hop_count * width // n_dom
+    strip = hidden // (n_dom * n_rep)
 
     out_share = outer_rows(act_mid, grad_logits).astype(jnp.bfloat16)
-    out_share = out_share.reshape(n_dom, n_rep, hidden // (n_dom * n_rep), classes)
-    out_share = lax.psum_scatter(out_share, "dom", scatter_dimension=0, tiled=False)
-    out_share = lax.psum_scatter(out_share, "rep", scatter_dimension=0, tiled=False)
+    out_pad = -classes % 256
+    out_share = jnp.pad(out_share, ((0, 0), (0, out_pad)))
     mid_share = outer_rows(act_first, grad_mid).astype(jnp.bfloat16)
-    mid_share = mid_share.reshape(n_dom, n_rep, hidden // (n_dom * n_rep), hidden)
-    mid_share = lax.psum_scatter(mid_share, "dom", scatter_dimension=0, tiled=False)
-    mid_share = lax.psum_scatter(mid_share, "rep", scatter_dimension=0, tiled=False)
+    upper = jnp.concatenate([mid_share, out_share], axis=1)
+    upper = upper.reshape(n_dom // 2, 2, n_rep, strip, hidden + classes + out_pad)
+    upper = halve(upper, "dom", 0, 1).astype(jnp.bfloat16)
+    upper = scatter_two_ways(upper.transpose(1, 0, 2, 3), dom_bits)
 
     grad_first = (inner_cols(grad_mid, mid_weight) * slope_first).astype(jnp.bfloat16)
-    first_parts = [
-        outer_rows(part, grad_first).astype(jnp.bfloat16).reshape(n_rep, width, hidden)
-        for part in columns
-    ]
-    first_share = jnp.concatenate(first_parts, axis=1)
-    quarter = hop_count * width // n_dom
-    first_share = share(first_share, 1)
+    first_parts = []
+    for part in columns:
+        piece = outer_rows(part, grad_first).astype(jnp.bfloat16)
+        piece = piece.reshape(n_rep, n_dom // (2 * hop_count), 2, quarter, hidden)
+        first_parts.append(halve(piece, "dom", 0, 2).astype(jnp.bfloat16))
+    lower = scatter_two_ways(jnp.concatenate(first_parts, axis=1), dom_bits)
     return (
-        first_share.astype(jnp.float32).reshape(1, quarter, hidden),
-        mid_share.astype(jnp.float32),
-        out_share.astype(jnp.float32),
+        lower.reshape(1, quarter, hidden),
+        upper[:, :hidden],
+        upper[:, hidden : hidden + classes],
     )
 
 

time: 465 us -> 301 us (0.65)
  waiting for transfers between devices: 170 us -> 67.1 us
  blocking collectives: 143 us -> 59.7 us
  local copies, waits for them, and re-layouts: 48.1 us -> 62.9 us
  between operations: 14.5 us -> 1.36 us
  starting transfers between devices: 14 us -> 26.6 us
  other arithmetic: 8.54 us -> 17 us
    reduce_scatter x6 -> x0, waiting for transfers between devices: 161 us -> none  [the longest x1 54.6 us: share(): part = lax.psum_scatter(full, 'dom', scatter_dimension=lead, tiled=True)]
    all_gather x1, blocking collectives: 83.5 us -> 8.45 us  [per_device(): lax.all_gather(jnp.concatenate([exported, part_labels], axis=0), 'dom')]
    ppermute x0 -> x21, waiting for transfers between devices: none -> 36.6 us  [halve(): came = lax.ppermute(sent, name, pairs)]
    all_to_all x3, waiting for transfers between devices: 9.44 us -> 30.4 us  [exchange_rows(): return lax.all_to_all(sent, 'rep', split_axis=0, concat_axis=0, tiled=True)]
    ppermute x0 -> x21, starting transfers between devices: none -> 13 us  [halve(): came = lax.ppermute(sent, name, pairs)]
    all_gather x3 -> x2, blocking collectives: 28.4 us -> 20.1 us  [per_device(): halo_rows = lax.all_gather(exported, 'dom', axis=0, tiled=True)]
    squeeze x0 -> x21, local copies, waits for them, and re-layouts: none -> 7.27 us  [halve(): sent = lax.dynamic_index_in_dim(part, 1 - mine, axis, keepdims=False)]
    transpose x4 -> x5, local copies, waits for them, and re-layouts: 8.2 us -> 10.4 us  [per_device(): moved[hop_index].transpose(1, 0, 2).reshape(batch_rows, n_rep * width)]
  transfers between devices with their start and end apart: 9 -> 24, of which waited for: 7 -> 15; matrix products, arithmetic and copies ran while one was open for 16% -> 27% of each run, Pallas kernels for 1% -> 0%
where the time goes in v2:
time: 301 us; the launch traced here: 300 us
  waiting for transfers between devices  67.1 us (22%)
  local copies, waits for them, and re-layouts  62.9 us (21%)
  blocking collectives  59.7 us (20%)
  matrix products  50.7 us (17%)
  starting transfers between devices  26.6 us (9%)
  other arithmetic  17 us (6%)
  Pallas kernels  14.4 us (5%)
    ppermute x21, waiting for transfers between devices, halve(): came = lax.ppermute(sent, name, pairs)  36.6 us
    all_to_all x1, blocking collectives, exchange_rows(): return lax.all_to_all(sent, 'rep', split_axis=0, concat_axis=0, tiled=True)  31.2 us
    all_to_all x3, waiting for transfers between devices, exchange_rows(): return lax.all_to_all(sent, 'rep', split_axis=0, concat_axis=0, tiled=True)  30.4 us
    gather x1, local copies, waits for them, and re-layouts, per_device(): picked_rows = train_rows[0][shuffle[0]] - lax.axis_index('rep') * batch_rows  23 us
    dot_general x4, matrix products, per_device(): term = jnp.dot(part, weight, preferred_element_type=jnp.float32)  20.7 us
    all_gather x2, blocking collectives, per_device(): halo_rows = lax.all_gather(exported, 'dom', axis=0, tiled=True)  20.1 us
    dot_general x7, matrix products, outer_rows(): lax.dot_general(left_side, right_side, (((0,), (0,)), ((), ())), preferre...  16.9 us
    pallas_call x3, Pallas kernels, propagate(): pl.pallas_call(hop_kernel, grid_spec=pltpu.PrefetchScalarGridSpec(num_sca...  14.4 us
  transfers between devices with their start and end apart: 24, of which 15 were waited for; matrix products, arithmetic and copies ran while one was open for 27% of the time, Pallas kernels for 0%

profile of v2, /device:TPU:0, one launch (start us, length us, event | category | flops | bytes accessed | tf_op | source)
XLA Modules:
  0.0 299.6 jit_solution(15096355996564076210)
XLA Ops:
  5.2 10.8 %all-gather.halo_ref = bf16[1024,128]{1,0:T(8,128)(2,1)S(1)} all-gather(bf16[128,128]{1,0:T(8,128)(2,1)S(1)} %gather_fusion.1), channel_id=2, replica_groups=mesh['dom'=8,'rep'=4] {'dom'}, dimensions={0}, use_global_device_ids=true | all-gather | bytes 294912 | tf_op jit(solution)/shard_map/all_gather | solution.py:198
  15.9 3.4 %copy-done.1 = bf16[32,8,128,128]{3,2,1,0:T(8,128)(2,1)S(1)} copy-done((bf16[32,8,128,128]{3,2,1,0:T(8,128)(2,1)S(1)}, bf16[32,8,128,128]{3,2,1,0:T(8,128)(2,1)}, u32[]{:S(2)}) %copy-start.1) | copy-done | bytes 8388632
  20.5 4.6 %propagate_hop.3 = (bf16[4096,128]{1,0:T(8,128)(2,1)S(1)}, bf16[128,128]{1,0:T(8,128)(2,1)S(1)}) custom-call(s32[32,8]{1,0:T(8,128)S(1)} %copy.50.columns, bf16[4096,128]{1,0:T(8,128)(2,1)S(1)} %copy-done.4, bf16[1024,128]{1,0:T(8,128)(2,1)S(1)} %all-gather.halo_ref, bf16[32,8,128,128]{3,2,1,0:T(8,128)(2,1)S(1)} %copy-done.1, ...), custom_call_target="tpu_custom_call" | custom-call | flops 1073741824 | bytes 12582912 | tf_op jit(solution)/shard_map/propagate_hop/pallas_call | solution.py:76
  25.1 9.3 %all_gather.13.halo_ref = bf16[1024,128]{1,0:T(8,128)(2,1)S(1)} all-gather(bf16[128,128]{1,0:T(8,128)(2,1)S(1)} %get-tuple-element.9), channel_id=1, replica_groups=mesh['dom'=8,'rep'=4] {'dom'}, dimensions={0}, use_global_device_ids=true | all-gather | bytes 294912 | tf_op jit(solution)/shard_map/all_gather | solution.py:198
  34.4 4.6 %propagate_hop.4 = (bf16[4096,128]{1,0:T(8,128)(2,1)S(1)}, bf16[128,128]{1,0:T(8,128)(2,1)S(1)}) custom-call(s32[32,8]{1,0:T(8,128)S(1)} %copy.50.columns, bf16[4096,128]{1,0:T(8,128)(2,1)S(1)} %get-tuple-element.8.hop_ref, bf16[1024,128]{1,0:T(8,128)(2,1)S(1)} %all_gather.13.halo_ref, bf16[32,8,128,128]{3,2,1,0:T(8,128)(2,1)S(1)} %copy-done.2, ...), custom_call_target="tpu_custom_call" | custom-call | flops 1073741824 | bytes 12582912 | tf_op jit(solution)/shard_map/propagate_hop/pallas_call | solution.py:76
  39.1 31.2 %all_to_all.20 = bf16[4,1024,128]{2,1,0:T(8,128)(2,1)} all-to-all(bf16[4,1024,128]{2,1,0:T(8,128)(2,1)S(1)} %bitcast.203), channel_id=1, replica_groups=mesh['dom'=8,'rep'=4] {'rep'}, dimensions={0} | all-to-all | bytes 2097152 | tf_op jit(solution)/shard_map/all_to_all | solution.py:113
  71.2 4.3 %all-to-all-start.1 = ((bf16[4,1024,128]{2,1,0:T(8,128)(2,1)}), bf16[4,1024,128]{2,1,0:T(8,128)(2,1)}, u32[]{:S(2)}, u32[]{:S(2)}) async-start(bf16[4,1024,128]{2,1,0:T(8,128)(2,1)} %bitcast.204), calls=%async_computation.1 | async-start | bytes 2097152 | tf_op jit(solution)/shard_map/all_to_all | solution.py:113
  77.8 23.1 %all-to-all-done.1 = bf16[4,1024,128]{2,1,0:T(8,128)(2,1)} async-done(((bf16[4,1024,128]{2,1,0:T(8,128)(2,1)}), bf16[4,1024,128]{2,1,0:T(8,128)(2,1)}, u32[]{:S(2)}, u32[]{:S(2)}) %all-to-all-start.1) | async-done | bytes 1048608 | tf_op jit(solution)/shard_map/all_to_all | solution.py:113
  100.9 4.3 %all-to-all-start = ((bf16[4,1040,128]{2,1,0:T(8,128)(2,1)}), bf16[4,1040,128]{2,1,0:T(8,128)(2,1)}, u32[]{:S(2)}, u32[]{:S(2)}) async-start(bf16[4,1040,128]{2,1,0:T(8,128)(2,1)} %pad_maximum_fusion.1), calls=%async_computation | async-start | bytes 2129920 | tf_op jit(solution)/shard_map/all_to_all | solution.py:113
  105.3 23.0 %gather_fusion = s32[4096]{0:T(1024)S(1)} fusion(s32[4096]{0:T(1024)S(1)} %bitcast.207, s32[4096]{0:T(1024)S(1)} %broadcast_clamp_fusion), kind=kCustom, calls=%fused_computation | custom fusion | bytes 49152 | tf_op jit(solution)/shard_map/gather | solution.py:210
  133.4 4.8 %fusion.28 = f32[1024,1024,1]{1,0,2:T(8,128)} fusion(bf16[4,512,1024]{2,1,0:T(8,128)(2,1)} %param.17, bf16[4,1024,128]{2,1,0:T(8,128)(2,1)} %all_to_all.20), kind=kOutput, calls=%fused_computation.61 | convolution fusion | flops 1073741824 | bytes 6291456 | tf_op jit(solution)/shard_map/dot_general | solution.py:228
  138.9 8.5 %all-gather.1 = bf16[1280,128]{1,0:T(8,128)(2,1)S(1)} all-gather(bf16[160,128]{1,0:T(8,128)(2,1)S(1)} %pad_maximum_fusion.3), channel_id=3, replica_groups=mesh['dom'=8,'rep'=4] {'dom'}, dimensions={0}, use_global_device_ids=true | all-gather | bytes 368640 | tf_op jit(solution)/shard_map/all_gather | solution.py:194
  152.0 5.2 %propagate_hop.5 = (bf16[4096,128]{1,0:T(8,128)(2,1)S(1)}, bf16[128,128]{1,0:T(8,128)(2,1)}) custom-call(s32[32,8]{1,0:T(8,128)S(1)} %copy.50.columns, bf16[4096,128]{1,0:T(8,128)(2,1)S(1)} %copy-done.6, bf16[1024,128]{1,0:T(8,128)(2,1)S(1)} %bitcast.206, bf16[32,8,128,128]{3,2,1,0:T(8,128)(2,1)S(1)} %copy-done.3, bf16[128,4096]{1,0:T(8,128)(2,1)S(1)} %fusion.19.pick_ref), custom_call_target="tpu_custom_call" | custom-call | flops 1073741824 | bytes 12582912 | tf_op jit(solution)/shard_map/propagate_hop/pallas_call | solution.py:76
  158.2 5.0 %all-to-all-start.3 = ((bf16[4,1024,128]{2,1,0:T(8,128)(2,1)}), bf16[4,1024,128]{2,1,0:T(8,128)(2,1)S(1)}, u32[]{:S(2)}, u32[]{:S(2)}) async-start(bf16[4,1024,128]{2,1,0:T(8,128)(2,1)} %bitcast.205), calls=%async_computation.3 | async-start | bytes 2097152 | tf_op jit(solution)/shard_map/all_to_all | solution.py:113
  163.2 4.8 %fusion.30 = f32[1024,1024,1]{1,0,2:T(8,128)} fusion(bf16[4,512,1024]{2,1,0:T(8,128)(2,1)} %param.17, bf16[4,1024,128]{2,1,0:T(8,128)(2,1)} %all-to-all-done.1), kind=kOutput, calls=%fused_computation.63 | convolution fusion | flops 1073741824 | bytes 6291456 | tf_op jit(solution)/shard_map/dot_general | solution.py:228
  172.7 4.6 %fusion.51 = (f32[1024]{0:T(1024)S(1)}, f32[1024,153]{0,1:T(8,128)}) fusion(s32[4096]{0:T(1024)S(1)} %bitcast.237, s32[4096]{0:T(1024)S(1)} %copy-done.23), kind=kOutput, calls=%fused_computation.132 | convolution fusion | flops 1288433664 | bytes 663552 | tf_op jit(solution)/shard_map/dot_general | solution.py:29
  177.3 4.9 %fusion.32 = f32[1024,1024,1]{1,0,2:T(8,128)} fusion(bf16[4,512,1024]{2,1,0:T(8,128)(2,1)} %param.17, bf16[4,1040,128]{2,1,0:T(8,128)(2,1)} %all-to-all-done), kind=kOutput, calls=%fused_computation.65 | convolution fusion | flops 1073741824 | bytes 6291456 | tf_op jit(solution)/shard_map/dot_general | solution.py:228
  182.1 7.3 %all-to-all-done.3 = bf16[4,1024,128]{2,1,0:T(8,128)(2,1)S(1)} async-done(((bf16[4,1024,128]{2,1,0:T(8,128)(2,1)}), bf16[4,1024,128]{2,1,0:T(8,128)(2,1)S(1)}, u32[]{:S(2)}, u32[]{:S(2)}) %all-to-all-start.3) | async-done | bytes 1048608 | tf_op jit(solution)/shard_map/all_to_all | solution.py:113
  189.5 6.3 %bitcast_add_fusion = f32[1024,1024]{1,0:T(8,128)S(1)} fusion(f32[1024,1024,1]{1,0,2:T(8,128)} %fusion.28, f32[1024,1024,1]{1,0,2:T(8,128)} %fusion.30, f32[1024,1024,1]{1,0,2:T(8,128)} %fusion.32, bf16[4,512,1024]{2,1,0:T(8,128)(2,1)} %param.17, bf16[4,1024,128]{2,1,0:T(8,128)(2,1)S(1)} %all-to-all-done.3), kind=kOutput, calls=%fused_computation.25 | convolution fusion | flops 1076887552 | bytes 18874368 | tf_op jit(solution)/shard_map/dot_general | solution.py:228
  195.8 3.5 %multiply_convert_fusion = (bf16[1024,1024]{1,0:T(8,128)(2,1)S(1)}, f32[1024,1024]{1,0:T(8,128)S(1)}) fusion(bf16[1024,1024]{1,0:T(8,128)(2,1)S(1)} %copy-done, f32[1024,1024]{1,0:T(8,128)S(1)} %bitcast_add_fusion), kind=kOutput, calls=%fused_computation.28 | convolution fusion | flops 2166358016 | bytes 12582912 | tf_op jit(solution)/shard_map/dot_general | solution.py:232
  206.7 5.6 %fusion.16 = bf16[1024,1024]{1,0:T(8,128)(2,1)} fusion(f32[1024,1024]{1,0:T(8,128)S(1)} %bitcast_add_fusion, bf16[1024,1024]{1,0:T(8,128)(2,1)S(1)} %fusion.11, bf16[1024,1024]{1,0:T(8,128)(2,1)S(1)} %copy-done), kind=kOutput, calls=%fused_computation.24 | convolution fusion | flops 2167406592 | bytes 10485760 | tf_op jit(solution)/shard_map/dot_general | solution.py:35
  214.0 4.4 %copy.60 = bf16[1024,1280]{1,0:T(8,128)(2,1)} copy(bf16[1024,1280]{0,1:T(8,128)(2,1)} %fusion.17) | data formatting | bytes 5242880 | tf_op jit(solution)/shard_map/concatenate | solution.py:250
  245.6 11.6 %collective-permute-done.4 = bf16[4,2,64,512]{3,2,1,0:T(8,128)(2,1)} collective-permute-done((bf16[4,2,64,512]{3,2,1,0:T(8,128)(2,1)}, bf16[4,2,64,512]{3,2,1,0:T(8,128)(2,1)}, u32[]{:S(2)}, u32[]{:S(2)}) %collective-permute-start.4) | collective-permute-done | bytes 524320 | tf_op jit(solution)/shard_map/ppermute | solution.py:122
  266.5 4.1 %collective-permute-done.9 = bf16[4,64,512]{2,1,0:T(8,128)(2,1)S(1)} collective-permute-done((bf16[4,64,512]{2,1,0:T(8,128)(2,1)S(1)}, bf16[4,64,512]{2,1,0:T(8,128)(2,1)S(1)}, u32[]{:S(2)}, u32[]{:S(2)}) %collective-permute-start.9) | collective-permute-done | bytes 262176 | tf_op jit(solution)/shard_map/ppermute | solution.py:122
  (174 shorter events, 99.3 us)
Async XLA Ops:
  71.2 29.7 %all-to-all-start.1 = ((bf16[4,1024,128]{2,1,0:T(8,128)(2,1)}), bf16[4,1024,128]{2,1,0:T(8,128)(2,1)}, u32[]{:S(2)}, u32[]{:S(2)}) async-start(bf16[4,1024,128]{2,1,0:T(8,128)(2,1)} %bitcast.204), calls=%async_computation.1 | async-start | bytes 2097152 | tf_op jit(solution)/shard_map/all_to_all | solution.py:113
  100.9 37.3 %all-to-all-start = ((bf16[4,1040,128]{2,1,0:T(8,128)(2,1)}), bf16[4,1040,128]{2,1,0:T(8,128)(2,1)}, u32[]{:S(2)}, u32[]{:S(2)}) async-start(bf16[4,1040,128]{2,1,0:T(8,128)(2,1)} %pad_maximum_fusion.1), calls=%async_computation | async-start | bytes 2129920 | tf_op jit(solution)/shard_map/all_to_all | solution.py:113
  158.2 31.3 %all-to-all-start.3 = ((bf16[4,1024,128]{2,1,0:T(8,128)(2,1)}), bf16[4,1024,128]{2,1,0:T(8,128)(2,1)S(1)}, u32[]{:S(2)}, u32[]{:S(2)}) async-start(bf16[4,1024,128]{2,1,0:T(8,128)(2,1)} %bitcast.205), calls=%async_computation.3 | async-start | bytes 2097152 | tf_op jit(solution)/shard_map/all_to_all | solution.py:113
  221.0 41.0 %collective-permute-start.12 = (bf16[4,4,32,1280]{3,2,1,0:T(8,128)(2,1)}, bf16[4,4,32,1280]{3,2,1,0:T(8,128)(2,1)}, u32[]{:S(2)}, u32[]{:S(2)}) collective-permute-start(bf16[4,4,32,1280]{3,2,1,0:T(8,128)(2,1)} %dynamic-slice_bitcast_fusion), channel_id=1, source_target_pairs={{0,4},{4,0},{8,12},{12,8},{16,20},{20,16},{24,28},{28,24},{1,5},{5... | collective-permute-start | bytes 3932168 | tf_op jit(solution)/shard_map/ppermute | solution.py:122
  226.1 10.2 %collective-permute-start = (bf16[4,1,64,1024]{3,2,1,0:T(8,128)(2,1)}, bf16[4,1,64,1024]{3,2,1,0:T(8,128)(2,1)}, u32[]{:S(2)}, u32[]{:S(2)}) collective-permute-start(bf16[4,1,64,1024]{3,2,1,0:T(8,128)(2,1)} %dynamic-slice_bitcast_fusion.6), channel_id=1, source_target_pairs={{0,4},{4,0},{8,12},{12,8},{16,20},{20,16},{24,28},{28,24},{1,5},{5... | collective-permute-start | bytes 1572872 | tf_op jit(solution)/shard_map/ppermute | solution.py:122
  228.7 8.9 %collective-permute-start.1 = (bf16[4,1,64,1024]{3,2,1,0:T(8,128)(2,1)}, bf16[4,1,64,1024]{3,2,1,0:T(8,128)(2,1)}, u32[]{:S(2)}, u32[]{:S(2)}) collective-permute-start(bf16[4,1,64,1024]{3,2,1,0:T(8,128)(2,1)} %dynamic-slice_bitcast_fusion.5), channel_id=1, source_target_pairs={{0,4},{4,0},{8,12},{12,8},{16,20},{20,16},{24,28},{28,24},{1,5},{5... | collective-permute-start | bytes 1572872 | tf_op jit(solution)/shard_map/ppermute | solution.py:122
  231.1 7.8 %collective-permute-start.2 = (bf16[4,1,64,1024]{3,2,1,0:T(8,128)(2,1)}, bf16[4,1,64,1024]{3,2,1,0:T(8,128)(2,1)}, u32[]{:S(2)}, u32[]{:S(2)}) collective-permute-start(bf16[4,1,64,1024]{3,2,1,0:T(8,128)(2,1)} %dynamic-slice_bitcast_fusion.4), channel_id=1, source_target_pairs={{0,4},{4,0},{8,12},{12,8},{16,20},{20,16},{24,28},{28,24},{1,5},{5... | collective-permute-start | bytes 1572872 | tf_op jit(solution)/shard_map/ppermute | solution.py:122
  236.1 4.1 %collective-permute-start.3 = (bf16[4,1,64,1024]{3,2,1,0:T(8,128)(2,1)S(1)}, bf16[4,1,64,1024]{3,2,1,0:T(8,128)(2,1)S(1)}, u32[]{:S(2)}, u32[]{:S(2)}) collective-permute-start(bf16[4,1,64,1024]{3,2,1,0:T(8,128)(2,1)S(1)} %dynamic-slice_bitcast_fusion.3), channel_id=1, source_target_pairs={{0,4},{4,0},{8,12},{12,8},{16,20},{20,16},{24,28},{28,24},{1,5},{5... | collective-permute-start | bytes 1572872 | tf_op jit(solution)/shard_map/ppermute | solution.py:122
  242.7 14.4 %collective-permute-start.4 = (bf16[4,2,64,512]{3,2,1,0:T(8,128)(2,1)}, bf16[4,2,64,512]{3,2,1,0:T(8,128)(2,1)}, u32[]{:S(2)}, u32[]{:S(2)}) collective-permute-start(bf16[4,2,64,512]{3,2,1,0:T(8,128)(2,1)} %dynamic-slice_bitcast_fusion.2), channel_id=1, source_target_pairs={{0,8},{4,12},{8,0},{12,4},{16,24},{20,28},{24,16},{28,20},{1,9},{5... | collective-permute-start | bytes 1572872 | tf_op jit(solution)/shard_map/ppermute | solution.py:122
  245.1 15.1 %collective-permute-start.8 = (bf16[4,2,64,512]{3,2,1,0:T(8,128)(2,1)}, bf16[4,2,64,512]{3,2,1,0:T(8,128)(2,1)}, u32[]{:S(2)}, u32[]{:S(2)}) collective-permute-start(bf16[4,2,64,512]{3,2,1,0:T(8,128)(2,1)} %dynamic-slice_bitcast_fusion.1), channel_id=1, source_target_pairs={{0,16},{4,20},{8,24},{12,28},{16,0},{20,4},{24,8},{28,12},{1,17},{... | collective-permute-start | bytes 1572872 | tf_op jit(solution)/shard_map/ppermute | solution.py:122
  258.6 7.8 %collective-permute-start.5 = (bf16[4,64,512]{2,1,0:T(8,128)(2,1)S(1)}, bf16[4,64,512]{2,1,0:T(8,128)(2,1)S(1)}, u32[]{:S(2)}, u32[]{:S(2)}) collective-permute-start(bf16[4,64,512]{2,1,0:T(8,128)(2,1)S(1)} %dynamic-slice_bitcast_fusion.10), channel_id=1, source_target_pairs={{0,16},{4,20},{8,24},{12,28},{16,0},{20,4},{24,8},{28,12},{1,17},{... | collective-permute-start | bytes 786440 | tf_op jit(solution)/shard_map/ppermute | solution.py:122
  261.3 9.3 %collective-permute-start.9 = (bf16[4,64,512]{2,1,0:T(8,128)(2,1)S(1)}, bf16[4,64,512]{2,1,0:T(8,128)(2,1)S(1)}, u32[]{:S(2)}, u32[]{:S(2)}) collective-permute-start(bf16[4,64,512]{2,1,0:T(8,128)(2,1)S(1)} %dynamic-slice_bitcast_fusion.9), channel_id=1, source_target_pairs={{0,8},{4,12},{8,0},{12,4},{16,24},{20,28},{24,16},{28,20},{1,9},{5... | collective-permute-start | bytes 786440 | tf_op jit(solution)/shard_map/ppermute | solution.py:122
  263.8 19.8 %collective-permute-start.13 = (bf16[4,2,32,640]{3,2,0,1:T(8,128)(2,1)S(1)}, bf16[4,2,32,640]{3,2,0,1:T(8,128)(2,1)S(1)}, u32[]{:S(2)}, u32[]{:S(2)}) collective-permute-start(bf16[4,2,32,640]{3,2,0,1:T(8,128)(2,1)S(1)} %dynamic-slice_bitcast_fusion.8), channel_id=1, source_target_pairs={{0,8},{4,12},{8,0},{12,4},{16,24},{20,28},{24,16},{28,20},{1,9},{5... | collective-permute-start | bytes 983048 | tf_op jit(solution)/shard_map/ppermute | solution.py:122
  265.4 16.6 %collective-permute-start.17 = (bf16[4,2,32,640]{3,2,0,1:T(8,128)(2,1)S(1)}, bf16[4,2,32,640]{3,2,0,1:T(8,128)(2,1)S(1)}, u32[]{:S(2)}, u32[]{:S(2)}) collective-permute-start(bf16[4,2,32,640]{3,2,0,1:T(8,128)(2,1)S(1)} %dynamic-slice_bitcast_fusion.7), channel_id=1, source_target_pairs={{0,16},{4,20},{8,24},{12,28},{16,0},{20,4},{24,8},{28,12},{1,17},{... | collective-permute-start | bytes 983048 | tf_op jit(solution)/shard_map/ppermute | solution.py:122
  266.4 6.3 %collective-permute-start.6 = (bf16[2,64,512]{2,1,0:T(8,128)(2,1)S(1)}, bf16[2,64,512]{2,1,0:T(8,128)(2,1)S(1)}, u32[]{:S(2)}, u32[]{:S(2)}) collective-permute-start(bf16[2,64,512]{2,1,0:T(8,128)(2,1)S(1)} %dynamic-slice_bitcast_fusion.14), channel_id=1, source_target_pairs={{0,1},{1,0},{2,3},{3,2},{4,5},{5,4},{6,7},{7,6},{8,9},{9,8},{10,11... | collective-permute-start | bytes 393224 | tf_op jit(solution)/shard_map/ppermute | solution.py:122
  270.8 5.0 %collective-permute-start.10 = (bf16[2,64,512]{2,1,0:T(8,128)(2,1)S(1)}, bf16[2,64,512]{2,1,0:T(8,128)(2,1)S(1)}, u32[]{:S(2)}, u32[]{:S(2)}) collective-permute-start(bf16[2,64,512]{2,1,0:T(8,128)(2,1)S(1)} %dynamic-slice_bitcast_fusion.13), channel_id=1, source_target_pairs={{0,1},{1,0},{2,3},{3,2},{4,5},{5,4},{6,7},{7,6},{8,9},{9,8},{10,11... | collective-permute-start | bytes 393224 | tf_op jit(solution)/shard_map/ppermute | solution.py:122
  272.7 6.1 %collective-permute-start.7 = (bf16[64,512]{1,0:T(8,128)(2,1)S(1)}, bf16[64,512]{1,0:T(8,128)(2,1)S(1)}, u32[]{:S(2)}, u32[]{:S(2)}) collective-permute-start(bf16[64,512]{1,0:T(8,128)(2,1)S(1)} %dynamic-slice_bitcast_fusion.18), channel_id=1, source_target_pairs={{0,2},{1,3},{2,0},{3,1},{4,6},{5,7},{6,4},{7,5},{8,10},{9,11},{10,... | collective-permute-start | bytes 196616 | tf_op jit(solution)/shard_map/ppermute | solution.py:122
  275.8 5.4 %collective-permute-start.11 = (bf16[64,512]{1,0:T(8,128)(2,1)S(1)}, bf16[64,512]{1,0:T(8,128)(2,1)S(1)}, u32[]{:S(2)}, u32[]{:S(2)}) collective-permute-start(bf16[64,512]{1,0:T(8,128)(2,1)S(1)} %dynamic-slice_bitcast_fusion.17), channel_id=1, source_target_pairs={{0,2},{1,3},{2,0},{3,1},{4,6},{5,7},{6,4},{7,5},{8,10},{9,11},{10,... | collective-permute-start | bytes 196616 | tf_op jit(solution)/shard_map/ppermute | solution.py:122
  282.1 5.4 %collective-permute-start.18 = (bf16[4,32,640]{2,1,0:T(8,128)(2,1)S(1)}, bf16[4,32,640]{2,1,0:T(8,128)(2,1)S(1)}, u32[]{:S(2)}, u32[]{:S(2)}) collective-permute-start(bf16[4,32,640]{2,1,0:T(8,128)(2,1)S(1)} %dynamic-slice_bitcast_fusion.11), channel_id=1, source_target_pairs={{0,8},{4,12},{8,0},{12,4},{16,24},{20,28},{24,16},{28,20},{1,9},{5... | collective-permute-start | bytes 491528 | tf_op jit(solution)/shard_map/ppermute | solution.py:122
  283.8 5.4 %collective-permute-start.14 = (bf16[4,32,640]{2,1,0:T(8,128)(2,1)S(1)}, bf16[4,32,640]{2,1,0:T(8,128)(2,1)S(1)}, u32[]{:S(2)}, u32[]{:S(2)}) collective-permute-start(bf16[4,32,640]{2,1,0:T(8,128)(2,1)S(1)} %dynamic-slice_bitcast_fusion.12), channel_id=1, source_target_pairs={{0,16},{4,20},{8,24},{12,28},{16,0},{20,4},{24,8},{28,12},{1,17},{... | collective-permute-start | bytes 491528 | tf_op jit(solution)/shard_map/ppermute | solution.py:122
  287.6 5.4 %collective-permute-start.19 = (bf16[2,32,640]{2,1,0:T(8,128)(2,1)S(1)}, bf16[2,32,640]{2,1,0:T(8,128)(2,1)S(1)}, u32[]{:S(2)}, u32[]{:S(2)}) collective-permute-start(bf16[2,32,640]{2,1,0:T(8,128)(2,1)S(1)} %dynamic-slice_bitcast_fusion.15), channel_id=1, source_target_pairs={{0,1},{1,0},{2,3},{3,2},{4,5},{5,4},{6,7},{7,6},{8,9},{9,8},{10,11... | collective-permute-start | bytes 245768 | tf_op jit(solution)/shard_map/ppermute | solution.py:122
  289.2 4.6 %collective-permute-start.15 = (bf16[2,32,640]{2,1,0:T(8,128)(2,1)S(1)}, bf16[2,32,640]{2,1,0:T(8,128)(2,1)S(1)}, u32[]{:S(2)}, u32[]{:S(2)}) collective-permute-start(bf16[2,32,640]{2,1,0:T(8,128)(2,1)S(1)} %dynamic-slice_bitcast_fusion.16), channel_id=1, source_target_pairs={{0,1},{1,0},{2,3},{3,2},{4,5},{5,4},{6,7},{7,6},{8,9},{9,8},{10,11... | collective-permute-start | bytes 245768 | tf_op jit(solution)/shard_map/ppermute | solution.py:122
  293.0 5.0 %collective-permute-start.20 = (bf16[32,640]{1,0:T(8,128)(2,1)S(1)}, bf16[32,640]{1,0:T(8,128)(2,1)S(1)}, u32[]{:S(2)}, u32[]{:S(2)}) collective-permute-start(bf16[32,640]{1,0:T(8,128)(2,1)S(1)} %dynamic-slice_bitcast_fusion.19), channel_id=1, source_target_pairs={{0,2},{1,3},{2,0},{3,1},{4,6},{5,7},{6,4},{7,5},{8,10},{9,11},{10,... | collective-permute-start | bytes 122888 | tf_op jit(solution)/shard_map/ppermute | solution.py:122
  293.9 5.0 %collective-permute-start.16 = (bf16[32,640]{1,0:T(8,128)(2,1)S(1)}, bf16[32,640]{1,0:T(8,128)(2,1)S(1)}, u32[]{:S(2)}, u32[]{:S(2)}) collective-permute-start(bf16[32,640]{1,0:T(8,128)(2,1)S(1)} %dynamic-slice_bitcast_fusion.20), channel_id=1, source_target_pairs={{0,2},{1,3},{2,0},{3,1},{4,6},{5,7},{6,4},{7,5},{8,10},{9,11},{10,... | collective-permute-start | bytes 122888 | tf_op jit(solution)/shard_map/ppermute | solution.py:122
  (26 other events, 466.9 us)
